TPU v7x, 32 devices: a whole 2x2x4 slice. The times are simulated.
32 devices in a mesh: tp: 8 (over y, x, core), sp: 4 (over z).
Axes of the slice: x: 2, y: 2, z: 4, core: 2. Of those that a mesh axis runs over, the one named last changes fastest.
Arguments:
- inputs: bfloat16 [256, 8192], P('tp', 'sp'), may hold values from -6 to 6
- out_grad: bfloat16 [256, 8192], P('sp', 'tp'), may hold values from -6 to 6
- gate_pre: bfloat16 [256, 28672], P(None, 'tp'), may hold values from -6 to 6
- up_pre: bfloat16 [256, 28672], P(None, 'tp'), may hold values from -6 to 6
- w_gate: bfloat16 [8192, 28672], P('sp', 'tp'), may hold values from -0.0625 to 0.0625
- w_up: bfloat16 [8192, 28672], P('sp', 'tp'), may hold values from -0.0625 to 0.0625
- w_down: bfloat16 [28672, 8192], P('tp', 'sp'), may hold values from -0.03125 to 0.03125
Outputs:
- grad_input: bfloat16 [256, 8192], P('tp', 'sp')
- grad_gate: bfloat16 [8192, 28672], P('sp', 'tp')
- grad_up: bfloat16 [8192, 28672], P('sp', 'tp')
- grad_down: bfloat16 [28672, 8192], P('tp', 'sp')
All inputs are finite; a program needn't handle non-finite values.
Results may differ from a plain program's by a relative error of at most 0.0049.
Values may be sent and summed in bfloat16 or wider, within the bound.
A program may use at most 192 MiB of HBM per device.

v0:
```python
import jax
import jax.numpy as jnp
from jax import lax
from jax.sharding import PartitionSpec as P


def swiglu_back(hidden_grad, gate_pre, up_pre):
    gate = gate_pre.astype(jnp.float32)
    upward = up_pre.astype(jnp.float32)
    sigmoid = jax.nn.sigmoid(gate)
    up_grad = (hidden_grad * gate * sigmoid).astype(jnp.bfloat16)
    gate_grad = (hidden_grad * upward * sigmoid * (1.0 + gate * (1.0 - sigmoid))).astype(
        jnp.bfloat16
    )
    return (gate_grad, up_grad)


def rows_times(grads, weight):
    return lax.dot_general(
        grads, weight, (((1,), (1,)), ((), ())), preferred_element_type=jnp.float32
    )


def per_device(inputs, out_grad, gate_pre, up_pre, w_gate, w_up, w_down):
    wide_rows = lax.all_gather(out_grad, "tp", axis=1, tiled=True)
    regrouped = lax.all_to_all(wide_rows, "sp", split_axis=1, concat_axis=0, tiled=True)
    gate = gate_pre.astype(jnp.float32)
    hidden = (gate * jax.nn.sigmoid(gate) * up_pre.astype(jnp.float32)).astype(jnp.bfloat16)
    grad_down = lax.dot_general(
        hidden, regrouped, (((0,), (0,)), ((), ())), preferred_element_type=jnp.float32
    ).astype(jnp.bfloat16)
    partial_grad = lax.dot_general(
        regrouped, w_down, (((1,), (1,)), ((), ())), preferred_element_type=jnp.float32
    )
    hidden_grad = lax.psum(partial_grad, "sp")
    gate_grad, up_grad = swiglu_back(hidden_grad, gate_pre, up_pre)
    dims = (((0,), (0,)), ((), ()))
    piece = lax.all_gather(inputs, "tp", axis=0, tiled=True)
    new_gate = lax.dot_general(piece, gate_grad, dims, preferred_element_type=jnp.float32)
    new_up = lax.dot_general(piece, up_grad, dims, preferred_element_type=jnp.float32)
    via_gate = lax.psum_scatter(
        rows_times(gate_grad, w_gate), "tp", scatter_dimension=0, tiled=True
    )
    via_up = lax.psum_scatter(rows_times(up_grad, w_up), "tp", scatter_dimension=0, tiled=True)
    total = via_gate + via_up
    return (
        total.astype(jnp.bfloat16),
        new_gate.astype(jnp.bfloat16),
        new_up.astype(jnp.bfloat16),
        grad_down,
    )


def solution(mesh):
    in_specs = (
        P("tp", "sp"),
        P("sp", "tp"),
        P(None, "tp"),
        P(None, "tp"),
        P("sp", "tp"),
        P("sp", "tp"),
        P("tp", "sp"),
    )
    out_specs = (P("tp", "sp"), P("sp", "tp"), P("sp", "tp"), P("tp", "sp"))
    return jax.shard_map(
        per_device, mesh=mesh, in_specs=in_specs, out_specs=out_specs, check_vma=False
    )
```

profile of v0, /device:TPU:0, one launch (start us, length us, event | category | flops | bytes accessed | tf_op | source)
XLA Modules:
  0.0 316.0 jit_solution(610266666883076665)
XLA Ops:
  7.2 0.0 all-gather.3.cloned.1.call-start
  7.2 0.7 all-gather.3.cloned.1.call-update
  7.9 0.0 all-reduce.2.cloned.1.call-start
  7.9 28.2 %all-gather.3.cloned.1.call-done = bf16[64,8192]{1,0:T(8,128)(2,1)} async-done(((bf16[64,1024]{1,0:T(8,128)(2,1)}), bf16[64,8192]{1,0:T(8,128)(2,1)}) %all-gather.3.cloned.1.call-update) | async-done | bytes 1048592 | tf_op jit(solution)/shard_map/all_gather | solution.py:25
  36.1 1.3 copy.23
  37.4 30.6 %all_to_all.19 = bf16[64,4,2048]{2,0,1:T(8,128)(2,1)S(1)} all-to-all(bf16[64,4,2048]{2,0,1:T(8,128)(2,1)S(1)} %bitcast.20), channel_id=1, replica_groups=mesh['tp'=8,'sp'=4] {'sp'}, dimensions={1} | all-to-all | bytes 2097152 | tf_op jit(solution)/shard_map/all_to_all | solution.py:26
  68.0 9.1 %fusion.17 = f32[256,3584]{1,0:T(8,128)} fusion(bf16[256,2048]{1,0:T(8,128)(2,1)S(1)} %bitcast.21, bf16[3584,2048]{1,0:T(8,128)(2,1)} %param.13), kind=kOutput, calls=%fused_computation.25 | convolution fusion | flops 3758096384 | bytes 19398656 | tf_op jit(solution)/shard_map/dot_general | solution.py:32
  77.1 0.0 all-reduce.2.cloned.1.call-update
  77.1 0.0 all-gather.5.cloned.1.call-start
  77.2 0.7 all-gather.5.cloned.1.call-update
  77.9 0.0 reduce-scatter.2.cloned.1.call-start
  77.9 135.5 %all-reduce.2.cloned.1.call-done = f32[256,3584]{1,0:T(8,128)} async-done(((f32[256,3584]{1,0:T(8,128)}), f32[256,3584]{1,0:T(8,128)}) %all-reduce.2.cloned.1.call-update) | async-done | bytes 3670032 | tf_op jit(solution)/shard_map/psum | solution.py:35
  213.5 4.6 %fusion.4 = bf16[256,3584]{1,0:T(8,128)(2,1)S(1)} fusion(f32[256,3584]{1,0:T(8,128)} %all-reduce.2.cloned.1.call-done, bf16[256,3584]{1,0:T(8,128)(2,1)} %param.10, bf16[256,3584]{1,0:T(8,128)(2,1)} %param.9), kind=kLoop, calls=%fused_computation.13 | loop fusion | flops 11010048 | bytes 9175040 | tf_op jit(solution)/shard_map/convert_element_type | solution.py:12
  218.1 8.9 %fusion.18 = f32[256,2048]{1,0:T(8,128)} fusion(bf16[256,3584]{1,0:T(8,128)(2,1)S(1)} %fusion.4, bf16[2048,3584]{1,0:T(8,128)(2,1)} %param.11), kind=kOutput, calls=%fused_computation.26 | convolution fusion | flops 3758096384 | bytes 18612224 | tf_op jit(solution)/shard_map/dot_general | solution.py:19
  227.1 12.9 %convolution_add_fusion = f32[256,2048]{1,0:T(8,128)} fusion(f32[256,2048]{1,0:T(8,128)} %fusion.18, bf16[2048,3584]{1,0:T(8,128)(2,1)} %param.12, f32[256,3584]{1,0:T(8,128)} %all-reduce.2.cloned.1.call-done, bf16[256,3584]{1,0:T(8,128)(2,1)} %param.9), kind=kOutput, calls=%fused_computation.21 | convolution fusion | flops 3765043200 | bytes 24379392 | tf_op jit(solution)/shard_map/dot_general | solution.py:19
  240.0 0.0 reduce-scatter.2.cloned.1.call-update
  240.0 10.3 %convolution_convert_fusion = bf16[3584,2048]{1,0:T(8,128)(2,1)} fusion(bf16[256,2048]{1,0:T(8,128)(2,1)S(1)} %bitcast.22, bf16[256,3584]{1,0:T(8,128)(2,1)} %param.10, bf16[256,3584]{1,0:T(8,128)(2,1)} %param.9), kind=kOutput, calls=%fused_computation | convolution fusion | flops 3772776448 | bytes 19398656 | tf_op jit(solution)/shard_map/dot_general | solution.py:29
  250.3 0.0 all-gather.5.cloned.1.call-done
  250.3 12.9 %fusion.1 = bf16[2048,3584]{0,1:T(8,128)(2,1)} fusion(bf16[256,2048]{1,0:T(8,128)(2,1)} %all-gather.5.cloned.1.call-done, f32[256,3584]{1,0:T(8,128)} %all-reduce.2.cloned.1.call-done, bf16[256,3584]{1,0:T(8,128)(2,1)} %param.9), kind=kOutput, calls=%fused_computation.4 | convolution fusion | flops 3771858944 | bytes 21233664 | tf_op jit(solution)/shard_map/dot_general | solution.py:40
  263.2 0.0 copy-start
  263.2 18.8 %copy.20 = bf16[2048,3584]{1,0:T(8,128)(2,1)} copy(bf16[2048,3584]{0,1:T(8,128)(2,1)} %fusion.1) | data formatting | bytes 29360128
  281.9 0.0 copy-done
  281.9 7.3 %fusion = bf16[2048,3584]{0,1:T(8,128)(2,1)} fusion(bf16[256,3584]{1,0:T(8,128)(2,1)S(1)} %fusion.4, bf16[256,2048]{1,0:T(8,128)(2,1)S(1)} %copy-done), kind=kOutput, calls=%fused_computation.3 | convolution fusion | flops 3765436416 | bytes 17563648 | tf_op jit(solution)/shard_map/dot_general | solution.py:39
  289.2 18.6 %copy.19 = bf16[2048,3584]{1,0:T(8,128)(2,1)} copy(bf16[2048,3584]{0,1:T(8,128)(2,1)} %fusion) | data formatting | bytes 29360128
  307.9 0.0 reduce-scatter.2.cloned.1.call-done
  307.9 1.6 convert_element_type.39
Async XLA Ops:
  7.2 29.0 %all-gather.3.cloned.1.call-start = ((), (), s32[]{:S(2)}) async-start(), calls=%async_computation.2 | async-start | bytes 1179648 | tf_op jit(solution)/shard_map/all_gather | solution.py:25
  7.9 205.6 %all-reduce.2.cloned.1.call-start = ((), (), s32[]{:S(2)}) async-start(), calls=%async_computation.3 | async-start | bytes 7340032 | tf_op jit(solution)/shard_map/psum | solution.py:35
  77.1 173.1 %all-gather.5.cloned.1.call-start = ((), (), s32[]{:S(2)}) async-start(), calls=%async_computation.4 | async-start | bytes 1179648 | tf_op jit(solution)/shard_map/all_gather | solution.py:38
  77.9 230.0 %reduce-scatter.2.cloned.1.call-start = ((), (), s32[]{:S(2)}) async-start(), calls=%async_computation.5 | async-start | bytes 2359296 | tf_op jit(solution)/shard_map/reduce_scatter | solution.py:41
  263.2 18.8 %copy-start = (bf16[256,2048]{1,0:T(8,128)(2,1)S(1)}, bf16[256,2048]{1,0:T(8,128)(2,1)}, u32[]{:S(2)}) copy-start(bf16[256,2048]{1,0:T(8,128)(2,1)} %all-gather.5.cloned.1.call-done) | copy-start | bytes 3145732
Sparse Core Ops, SparseCore 0:
  9.9 26.1 all-gather.2
  77.3 136.1 all-reduce.1
  215.4 22.4 all-gather.4
  241.0 41.1 reduce-scatter.1
where the time goes:
time: 317 us; the launch traced here: 316 us
  waiting for transfers between devices  165 us (52%)
  matrix products  61.5 us (19%)
  local copies, waits for them, and re-layouts  38.7 us (12%)
  blocking collectives  30.6 us (10%)
  between operations  13.8 us (4%)
  other arithmetic  6.26 us (2%)
    psum x1, waiting for transfers between devices, per_device(): hidden_grad = lax.psum(partial_grad, 'sp')  136 us
    unnamed x4, local copies, waits for them, and re-layouts  37.4 us
    all_to_all x1, blocking collectives, per_device(): lax.all_to_all(wide_rows, 'sp', split_axis=1, concat_axis=0, tiled=True)  30.6 us
    all_gather x1, waiting for transfers between devices, per_device(): wide_rows = lax.all_gather(out_grad, 'tp', axis=1, tiled=True)  28.2 us
    dot_general x2, matrix products, rows_times(): lax.dot_general(grads, weight, (((1,), (1,)), ((), ())), preferred_elemen...  21.9 us
    dot_general x1, matrix products, per_device(): lax.dot_general(piece, up_grad, dims, preferred_element_type=jnp.float32)  12.9 us
    dot_general x1, matrix products, per_device(): lax.dot_general(hidden, regrouped, (((0,), (0,)), ((), ())), preferred_el...  10.3 us
    dot_general x1, matrix products, per_device(): lax.dot_general(regrouped, w_down, (((1,), (1,)), ((), ())), preferred_el...  9.13 us
  transfers between devices with their start and end apart: 4, of which 2 were waited for; matrix products, arithmetic and copies ran while one was open for 30% of the time, Pallas kernels for 0%

commit v1 on v0

v1 whole, which is shorter than its diff:
```python
import functools

import jax
import jax.numpy as jnp
from jax import lax
from jax.experimental import pallas as pl
from jax.experimental.pallas import tpu as pltpu
from jax.sharding import PartitionSpec as P

BF = jnp.bfloat16
F32 = jnp.float32
MESH = pl.DeviceIdType.MESH
ANY = pl.BlockSpec(memory_space=pl.ANY)
VM = pl.BlockSpec(memory_space=pltpu.VMEM)
SLOTS = 4


def swiglu_back(hidden_grad, gate_pre, up_pre):
    gate = gate_pre.astype(F32)
    upward = up_pre.astype(F32)
    sigmoid = jax.nn.sigmoid(gate)
    up_grad = (hidden_grad * gate * sigmoid).astype(BF)
    gate_grad = (hidden_grad * upward * sigmoid * (1.0 + gate * (1.0 - sigmoid))).astype(BF)
    return (gate_grad, up_grad)


def rows_times(grads, weight):
    return lax.dot_general(grads, weight, (((1,), (1,)), ((), ())), preferred_element_type=F32)


def plain(inputs, out_grad, gate_pre, up_pre, w_gate, w_up, w_down):
    wide_rows = lax.all_gather(out_grad, "tp", axis=1, tiled=True)
    regrouped = lax.all_to_all(wide_rows, "sp", split_axis=1, concat_axis=0, tiled=True)
    gate = gate_pre.astype(F32)
    hidden = (gate * jax.nn.sigmoid(gate) * up_pre.astype(F32)).astype(BF)
    grad_down = lax.dot_general(
        hidden, regrouped, (((0,), (0,)), ((), ())), preferred_element_type=F32
    ).astype(BF)
    partial_grad = rows_times(regrouped, w_down)
    hidden_grad = lax.psum(partial_grad, "sp")
    gate_grad, up_grad = swiglu_back(hidden_grad, gate_pre, up_pre)
    dims = (((0,), (0,)), ((), ()))
    piece = lax.all_gather(inputs, "tp", axis=0, tiled=True)
    new_gate = lax.dot_general(piece, gate_grad, dims, preferred_element_type=F32)
    new_up = lax.dot_general(piece, up_grad, dims, preferred_element_type=F32)
    via_gate = lax.psum_scatter(
        rows_times(gate_grad, w_gate), "tp", scatter_dimension=0, tiled=True
    )
    via_up = lax.psum_scatter(rows_times(up_grad, w_up), "tp", scatter_dimension=0, tiled=True)
    total = via_gate + via_up
    return (total.astype(BF), new_gate.astype(BF), new_up.astype(BF), grad_down)


def first_kernel(
    n_q, n_s, chunk, n_c, tile,
    inputs, out_grad, gate_pre, up_pre, w_gate, w_up, w_down,
    grad_in, x_out, in_t_out, gg_out, ug_out, hid_out,
    quarter, x_all, x_flat, in_all, in_t, w_d, w_gu, part,
    from_l, from_r, to_r, to_l, gates, ups, gg, ug, hid, g_in, half_in, block_out, block_in,
    sem_a, sem_b, sem_c, sem_d, sem_i, sem_j, sem_h, sem_e,
    sem_wd, sem_w, sem_gu, sem_r, sem_l, sem_out, sem_x,
):
    t = lax.axis_index("tp")
    s = lax.axis_index("sp")
    q = t // 2
    k = lax.rem(t, 2)
    mate = t + 1 - 2 * k
    rows16 = quarter.shape[1]
    half = quarter.shape[2]
    depth = x_flat.shape[1]
    tokens = x_flat.shape[0]
    cols = pl.ds(pl.multiple_of(k * half, half), half)

    def wd_copy(j):
        return pltpu.make_async_copy(
            w_down.at[pl.ds(pl.multiple_of(j * chunk, chunk), chunk)], w_d.at[j], sem_wd.at[j]
        )

    def col(j):
        return pl.ds(pl.multiple_of(j * chunk, chunk), chunk)

    def w_copies(j):
        slot = lax.rem(j, SLOTS)
        return (
            pltpu.make_async_copy(
                w_gate.at[:, col(j)], w_gu.at[slot, :, pl.ds(0, chunk)], sem_w.at[0, slot]
            ),
            pltpu.make_async_copy(
                w_up.at[:, col(j)], w_gu.at[slot, :, pl.ds(chunk, chunk)], sem_w.at[1, slot]
            ),
        )

    def pre_copies(j):
        return (
            pltpu.make_async_copy(gate_pre.at[:, col(j)], gates.at[j], sem_gu.at[0, j]),
            pltpu.make_async_copy(up_pre.at[:, col(j)], ups.at[j], sem_gu.at[1, j]),
        )

    def out_copies(j):
        return (
            pltpu.make_async_copy(gg.at[j], gg_out.at[j], sem_out.at[0, j]),
            pltpu.make_async_copy(ug.at[j], ug_out.at[j], sem_out.at[1, j]),
            pltpu.make_async_copy(hid.at[j], hid_out.at[j], sem_out.at[2, j]),
        )

    def remote(src, dst, sems, at, where):
        return pltpu.make_async_remote_copy(
            src_ref=src, dst_ref=dst, send_sem=sems.at[(0, *at)], recv_sem=sems.at[(1, *at)],
            device_id=where, device_id_type=MESH,
        )

    barrier = pltpu.get_barrier_semaphore()
    for o in range(1, n_q):
        pl.semaphore_signal(
            barrier, inc=1, device_id={"tp": lax.rem(q + o, n_q) * 2 + k}, device_id_type=MESH
        )
    for o in range(1, n_s):
        pl.semaphore_signal(
            barrier, inc=1, device_id={"sp": lax.rem(s + o, n_s)}, device_id_type=MESH
        )
    pl.semaphore_signal(barrier, inc=1, device_id={"tp": mate}, device_id_type=MESH)

    @pl.loop(0, n_c)
    def _(j):
        wd_copy(j).start()

    pl.semaphore_wait(barrier, n_q + n_s - 1)

    stage = []
    for o in range(1, n_q):
        peer = lax.rem(q + o, n_q)
        stage.append(
            remote(
                out_grad.at[pl.ds(pl.multiple_of(peer * rows16, rows16), rows16)],
                quarter.at[q], sem_a, (o,), {"tp": peer * 2 + k},
            )
        )
        stage[-1].start()
    quarter[q] = out_grad[pl.ds(pl.multiple_of(q * rows16, rows16), rows16), :]
    for c in stage:
        c.wait()
    stage = []
    for o in range(1, n_s):
        peer = lax.rem(s + o, n_s)
        stage.append(
            remote(quarter.at[peer], x_all.at[s, q, :, cols], sem_b, (o,), {"sp": peer})
        )
        stage[-1].start()
    x_all[s, q, :, cols] = quarter[s]
    for c in stage:
        c.wait()
    stage = []
    for o in range(1, n_q):
        peer = lax.rem(q + o, n_q)
        stage.append(
            remote(
                x_all.at[:, q, :, cols], x_all.at[:, q, :, cols], sem_c, (o,),
                {"tp": peer * 2 + k},
            )
        )
        stage[-1].start()

    @pl.loop(0, n_c)
    def _(j):
        for c in pre_copies(j):
            c.start()

    for j in range(min(SLOTS, n_c)):
        for c in w_copies(j):
            c.start()
    for c in stage:
        c.wait()
    swap = remote(x_all.at[:, :, :, cols], x_all.at[:, :, :, cols], sem_d, (0,), {"tp": mate})
    swap.start()
    in_stage = []
    for o in range(1, n_q):
        peer = lax.rem(q + o, n_q)
        in_stage.append(
            remote(inputs, in_all.at[q, k], sem_i, (o,), {"tp": peer * 2 + k})
        )
        in_stage[-1].start()
    in_all[q, k] = inputs[...]
    g_in[...] = jnp.zeros_like(g_in)
    swap.wait()
    x_flat[...] = x_all[...].reshape(tokens, depth)
    x_copy = pltpu.make_async_copy(x_flat, x_out, sem_x.at[0])
    x_copy.start()

    def send_r(j):
        return remote(
            to_r.at[j], from_l.at[j], sem_r, (j,), {"sp": jnp.minimum(s + 1, n_s - 1)}
        )

    def send_l(j):
        return remote(to_l.at[j], from_r.at[j], sem_l, (j,), {"sp": jnp.maximum(s - 1, 0)})

    @pl.loop(0, n_c)
    def _(j):
        wd_copy(j).wait()
        p = lax.dot_general(
            x_flat[...], w_d[j], (((1,), (1,)), ((), ())), preferred_element_type=F32
        )
        part[j] = p

        @pl.when(s == 0)
        def _():
            to_r[j] = p.astype(BF)
            send_r(j).start()
            from_l[j] = jnp.zeros((tokens, chunk), BF)

        @pl.when(s == n_s - 1)
        def _():
            to_l[j] = p.astype(BF)
            send_l(j).start()
            from_r[j] = jnp.zeros((tokens, chunk), BF)

    for c in in_stage:
        c.wait()
    in_swap = remote(in_all.at[:, k], in_all.at[:, k], sem_j, (0,), {"tp": mate})
    in_swap.start()

    lag = jnp.maximum(s - 1, n_s - 2 - s)

    def finish(f):
        for c in pre_copies(f):
            c.wait()
        h = part[f] + from_l[f].astype(F32) + from_r[f].astype(F32)
        gate = gates[f].astype(F32)
        upward = ups[f].astype(F32)
        sigmoid = 1.0 / (1.0 + jnp.exp(-gate))
        swish = gate * sigmoid
        gg[f] = (h * upward * sigmoid * (1.0 + gate * (1.0 - sigmoid))).astype(BF)
        ug[f] = (h * swish).astype(BF)
        hid[f] = (swish * upward).astype(BF).T
        for c in out_copies(f):
            c.start()
        for c in w_copies(f):
            c.wait()
        slot = lax.rem(f, SLOTS)

        @pl.loop(0, depth // tile)
        def _(i):
            at = pl.ds(pl.multiple_of(i * tile, tile), tile)
            w = w_gu[slot, at, :]
            d = lax.dot_general(
                gg[f], w[:, :chunk], (((1,), (1,)), ((), ())), preferred_element_type=F32
            ) + lax.dot_general(
                ug[f], w[:, chunk:], (((1,), (1,)), ((), ())), preferred_element_type=F32
            )
            g_in[:, :, :, at] += d.reshape(n_q, 2, tokens // (2 * n_q), tile)

        @pl.when(f + SLOTS < n_c)
        def _():
            for c in w_copies(f + SLOTS):
                c.start()

    @pl.loop(0, n_c + n_s - 2)
    def _(step):
        cr = step - (s - 1)
        cl = step - (n_s - 2 - s)
        f = step - lag

        @pl.when((s > 0) & (cr >= 0) & (cr < n_c))
        def _():
            send_r(cr).wait_recv()

            @pl.when(s < n_s - 1)
            def _():
                to_r[cr] = (part[cr] + from_l[cr].astype(F32)).astype(BF)
                send_r(cr).start()

        @pl.when((s < n_s - 1) & (cl >= 0) & (cl < n_c))
        def _():
            send_l(cl).wait_recv()

            @pl.when(s > 0)
            def _():
                to_l[cl] = (part[cl] + from_r[cl].astype(F32)).astype(BF)
                send_l(cl).start()

        @pl.when((f >= 0) & (f < n_c))
        def _():
            finish(f)

        @pl.when(step == n_c // 2)
        def _():
            in_swap.wait()
            in_t[...] = in_all[...].reshape(tokens, depth).T
            pltpu.make_async_copy(in_t, in_t_out, sem_x.at[1]).start()

    pair = remote(g_in.at[:, 1 - k], half_in, sem_h, (0,), {"tp": mate})
    pair.start()
    pair.wait()
    stage = []
    for o in range(1, n_q):
        peer = lax.rem(q + o, n_q)
        block_out[o] = (g_in[peer, k] + half_in[peer]).astype(BF)
        stage.append(
            remote(block_out.at[o], block_in.at[o], sem_e, (o,), {"tp": peer * 2 + k})
        )
        stage[-1].start()
    total = g_in[q, k] + half_in[q]

    @pl.loop(0, n_c)
    def _(j):
        for c in out_copies(j):
            c.wait()

        @pl.when(s < n_s - 1)
        def _():
            send_r(j).wait_send()

        @pl.when(s > 0)
        def _():
            send_l(j).wait_send()

    x_copy.wait()
    pltpu.make_async_copy(in_t, in_t_out, sem_x.at[1]).wait()
    for c in stage:
        c.wait()
    for o in range(1, n_q):
        total = total + block_in[o].astype(F32)
    grad_in[...] = total.astype(BF)


def second_kernel(n_sub, chunk, x, in_t, gg, ug, hid, d_gate, d_up, d_down):
    for c in range(n_sub):
        at = slice(c * chunk, (c + 1) * chunk)
        d_gate[:, at] = jnp.dot(in_t[...], gg[c], preferred_element_type=F32).astype(BF)
        d_up[:, at] = jnp.dot(in_t[...], ug[c], preferred_element_type=F32).astype(BF)
        d_down[at, :] = jnp.dot(hid[c], x[...], preferred_element_type=F32).astype(BF)


def fused(n_q, n_s, chunk, inputs, out_grad, gate_pre, up_pre, w_gate, w_up, w_down):
    rows, depth = inputs.shape
    tokens, units = gate_pre.shape
    n_c = units // chunk
    half = depth // 2
    rows16 = out_grad.shape[0] // n_q
    tile = min(512, depth)
    sds = jax.ShapeDtypeStruct
    dma = pltpu.SemaphoreType.DMA
    vm = pltpu.VMEM
    scratch = [
        vm((n_q, rows16, half), BF),
        vm((n_s, n_q, rows16, depth), BF),
        vm((tokens, depth), BF),
        vm((n_q, 2, rows, depth), BF),
        vm((depth, tokens), BF),
        vm((n_c, chunk, depth), BF),
        vm((SLOTS, depth, 2 * chunk), BF),
        vm((n_c, tokens, chunk), F32),
        vm((n_c, tokens, chunk), BF),
        vm((n_c, tokens, chunk), BF),
        vm((n_c, tokens, chunk), BF),
        vm((n_c, tokens, chunk), BF),
        vm((n_c, tokens, chunk), BF),
        vm((n_c, tokens, chunk), BF),
        vm((n_c, tokens, chunk), BF),
        vm((n_c, tokens, chunk), BF),
        vm((n_c, chunk, tokens), BF),
        vm((n_q, 2, rows, depth), F32),
        vm((n_q, rows, depth), F32),
        vm((n_q, rows, depth), BF),
        vm((n_q, rows, depth), BF),
        dma((2, n_q)),
        dma((2, n_s)),
        dma((2, n_q)),
        dma((2, 1)),
        dma((2, n_q)),
        dma((2, 1)),
        dma((2, 1)),
        dma((2, n_q)),
        dma((n_c,)),
        dma((2, SLOTS)),
        dma((2, n_c)),
        dma((2, n_c)),
        dma((2, n_c)),
        dma((3, n_c)),
        dma((2,)),
    ]
    grad_in, x, in_t, gg, ug, hid = pl.pallas_call(
        functools.partial(first_kernel, n_q, n_s, chunk, n_c, tile),
        out_shape=(
            sds((rows, depth), BF),
            sds((tokens, depth), BF),
            sds((depth, tokens), BF),
            sds((n_c, tokens, chunk), BF),
            sds((n_c, tokens, chunk), BF),
            sds((n_c, chunk, tokens), BF),
        ),
        in_specs=[VM, VM, ANY, ANY, ANY, ANY, ANY],
        out_specs=(VM, ANY, ANY, ANY, ANY, ANY),
        scratch_shapes=scratch,
        compiler_params=pltpu.CompilerParams(
            collective_id=0, has_side_effects=True, vmem_limit_bytes=60 * 1024 * 1024
        ),
        cost_estimate=pl.CostEstimate(
            flops=6 * tokens * depth * units,
            bytes_accessed=6 * depth * units + 14 * tokens * units,
            transcendentals=tokens * units,
        ),
    )(inputs, out_grad, gate_pre, up_pre, w_gate, w_up, w_down)

    n_sub = 2 if n_c % 2 == 0 else 1
    wide = n_sub * chunk
    whole = lambda i: (0, 0)
    d_gate, d_up, d_down = pl.pallas_call(
        functools.partial(second_kernel, n_sub, chunk),
        grid=(n_c // n_sub,),
        out_shape=(
            sds((depth, units), BF),
            sds((depth, units), BF),
            sds((units, depth), BF),
        ),
        in_specs=[
            pl.BlockSpec((tokens, depth), whole),
            pl.BlockSpec((depth, tokens), whole),
            pl.BlockSpec((n_sub, tokens, chunk), lambda i: (i, 0, 0)),
            pl.BlockSpec((n_sub, tokens, chunk), lambda i: (i, 0, 0)),
            pl.BlockSpec((n_sub, chunk, tokens), lambda i: (i, 0, 0)),
        ],
        out_specs=(
            pl.BlockSpec((depth, wide), lambda i: (0, i)),
            pl.BlockSpec((depth, wide), lambda i: (0, i)),
            pl.BlockSpec((wide, depth), lambda i: (i, 0)),
        ),
        compiler_params=pltpu.CompilerParams(vmem_limit_bytes=60 * 1024 * 1024),
        cost_estimate=pl.CostEstimate(
            flops=6 * tokens * depth * units,
            bytes_accessed=6 * depth * units + 6 * tokens * units,
            transcendentals=0,
        ),
    )(x, in_t, gg, ug, hid)
    return grad_in, d_gate, d_up, d_down


def per_device(n_t, n_s, chunk, *args):
    inputs, out_grad, gate_pre = args[:3]
    rows, depth = inputs.shape
    tokens, units = gate_pre.shape
    n_q = n_t // 2
    fits = (
        n_t % 2 == 0
        and n_q == n_s
        and n_s > 1
        and depth % 256 == 0
        and out_grad.shape == (tokens // n_s, depth // 2)
        and out_grad.shape[0] % (16 * n_q) == 0
        and rows % 16 == 0
        and units % chunk == 0
        and units // chunk > 3
        and units * depth <= 8 * 1024 * 1024
        and tokens * units <= 1024 * 1024
    )
    if fits:
        return fused(n_q, n_s, chunk, *args)
    return plain(*args)


def solution(mesh, chunk=256):
    in_specs = (
        P("tp", "sp"),
        P("sp", "tp"),
        P(None, "tp"),
        P(None, "tp"),
        P("sp", "tp"),
        P("sp", "tp"),
        P("tp", "sp"),
    )
    out_specs = (P("tp", "sp"), P("sp", "tp"), P("sp", "tp"), P("tp", "sp"))
    return jax.shard_map(
        functools.partial(per_device, mesh.shape["tp"], mesh.shape["sp"], chunk),
        mesh=mesh, in_specs=in_specs, out_specs=out_specs, check_vma=False,
    )
```

time: 317 us -> 119 us (0.38)
  waiting for transfers between devices: 165 us -> 0 us
  Pallas kernels: 0 us -> 117 us
  matrix products: 61.5 us -> 0 us
  local copies, waits for them, and re-layouts: 38.7 us -> 0.66 us
  blocking collectives: 30.6 us -> 0 us
  between operations: 13.8 us -> 0.65 us
  other arithmetic: 6.26 us -> 0 us
    psum x1 -> x0, waiting for transfers between devices: 136 us -> none  [per_device(): hidden_grad = lax.psum(partial_grad, 'sp')]
    pallas_call x0 -> x2, Pallas kernels: none -> 117 us  [the longest x1 98.5 us: fused(): pl.pallas_call(functools.partial(first_kernel, n_q, n_s, chunk, n_c, tile...]
    dot_general x6 -> x0, matrix products: 61.5 us -> none  [the longest x2 21.9 us: rows_times(): lax.dot_general(grads, weight, (((1,), (1,)), ((), ())), preferred_elemen...]
    unnamed x4 -> x3, local copies, waits for them, and re-layouts: 37.4 us -> 0.66 us
    all_to_all x1 -> x0, blocking collectives: 30.6 us -> none  [per_device(): lax.all_to_all(wide_rows, 'sp', split_axis=1, concat_axis=0, tiled=True)]
    all_gather x2 -> x0, waiting for transfers between devices: 28.2 us -> none  [the longest x1 28.2 us: per_device(): wide_rows = lax.all_gather(out_grad, 'tp', axis=1, tiled=True)]
    convert_element_type x2 -> x0, other arithmetic: 6.26 us -> none  [the longest x1 4.64 us: swiglu_back(): (hidden_grad * upward * sigmoid * (1.0 + gate * (1.0 - sigmoid))).astype(...]
  transfers between devices with their start and end apart: 4 -> 0, of which waited for: 2 -> 0; matrix products, arithmetic and copies ran while one was open for 30% -> 0% of each run, Pallas kernels for 0% -> 0%
where the time goes in v1:
time: 119 us; the launch traced here: 118 us
  Pallas kernels  117 us (98%)
    pallas_call x1, Pallas kernels, fused(): pl.pallas_call(functools.partial(first_kernel, n_q, n_s, chunk, n_c, tile...  98.5 us
    pallas_call x1, Pallas kernels, fused(): pl.pallas_call(functools.partial(second_kernel, n_sub, chunk), grid=(n_c...  18.6 us

profile of v1, /device:TPU:0, one launch (start us, length us, event | category | flops | bytes accessed | tf_op | source)
XLA Modules:
  0.0 118.4 jit_solution(95994100512896117)
XLA Ops:
  0.6 98.5 %shard_map.102 = (bf16[32,2048]{1,0:T(8,128)(2,1)}, bf16[256,2048]{1,0:T(8,128)(2,1)}, bf16[2048,256]{1,0:T(8,128)(2,1)}, bf16[14,256,256]{2,1,0:T(8,128)(2,1)},...) custom-call(bf16[32,2048]{1,0:T(8,128)(2,1)} %inputs.1, bf16[64,1024]{1,0:T(8,128)(2,1)} %out_grad.1, ...), custom_call_target="tpu_custom_call" | custom-call | flops 11274289152 | bytes 56885248 | tf_op jit(solution)/shard_map/pallas_call | solution.py:382
  99.1 0.0 copy-start
  99.1 18.6 %shard_map.103 = (bf16[2048,3584]{1,0:T(8,128)(2,1)}, bf16[2048,3584]{1,0:T(8,128)(2,1)}, bf16[3584,2048]{1,0:T(8,128)(2,1)}) custom-call(bf16[256,2048]{1,0:T(8,128)(2,1)} %get-tuple-element.14.x, bf16[2048,256]{1,0:T(8,128)(2,1)} %get-tuple-element.15.in_t, bf16[14,256,256]{2,1,0:T(8,128)(2,1)} %get-tuple-element.16.gg, ...), custom_call_target="tpu_custom_call" | custom-call | flops 11274289152 | bytes 49545216 | tf_op jit(solution)/shard_map/pallas_call | solution.py:408
  117.7 0.0 copy-done
  117.7 0.7 copy.12
Async XLA Ops:
  99.1 18.6 %copy-start = (bf16[32,2048]{1,0:T(8,128)(2,1)S(1)}, bf16[32,2048]{1,0:T(8,128)(2,1)}, u32[]{:S(2)}) copy-start(bf16[32,2048]{1,0:T(8,128)(2,1)} %get-tuple-element.26) | copy-start | bytes 393220

commit v2 on v1

--- a/solution.py
+++ b/solution.py
@@ -13,6 +13,7 @@
 ANY = pl.BlockSpec(memory_space=pl.ANY)
 VM = pl.BlockSpec(memory_space=pltpu.VMEM)
 SLOTS = 4
+SLACK = 2
 
 
 def swiglu_back(hidden_grad, gate_pre, up_pre):
@@ -56,7 +57,7 @@
     inputs, out_grad, gate_pre, up_pre, w_gate, w_up, w_down,
     grad_in, x_out, in_t_out, gg_out, ug_out, hid_out,
     quarter, x_all, x_flat, in_all, in_t, w_d, w_gu, part,
-    from_l, from_r, to_r, to_l, gates, ups, gg, ug, hid, g_in, half_in, block_out, block_in,
+    from_l, from_r, to_r, to_l, gates, ups, swishes, slopes, gg, ug, hid, g_in, half_in, block_out, block_in,
     sem_a, sem_b, sem_c, sem_d, sem_i, sem_j, sem_h, sem_e,
     sem_wd, sem_w, sem_gu, sem_r, sem_l, sem_out, sem_x,
 ):
@@ -100,8 +101,10 @@
         return (
             pltpu.make_async_copy(gg.at[j], gg_out.at[j], sem_out.at[0, j]),
             pltpu.make_async_copy(ug.at[j], ug_out.at[j], sem_out.at[1, j]),
-            pltpu.make_async_copy(hid.at[j], hid_out.at[j], sem_out.at[2, j]),
-        )
+        )
+
+    def hid_copy(j):
+        return pltpu.make_async_copy(hid.at[j], hid_out.at[j], sem_out.at[2, j])
 
     def remote(src, dst, sems, at, where):
         return pltpu.make_async_remote_copy(
@@ -124,7 +127,24 @@
     def _(j):
         wd_copy(j).start()
 
+    @pl.loop(0, n_c)
+    def _(j):
+        for c in pre_copies(j):
+            c.start()
+
     pl.semaphore_wait(barrier, n_q + n_s - 1)
+
+    def factors(f):
+        for c in pre_copies(f):
+            c.wait()
+        gate = gates[f].astype(F32)
+        upward = ups[f].astype(F32)
+        sigmoid = 1.0 / (1.0 + jnp.exp(-gate))
+        swish = gate * sigmoid
+        swishes[f] = swish
+        slopes[f] = upward * sigmoid * (1.0 + gate * (1.0 - sigmoid))
+        hid[f] = (swish * upward).astype(BF).T
+        hid_copy(f).start()
 
     stage = []
     for o in range(1, n_q):
@@ -147,6 +167,7 @@
         )
         stage[-1].start()
     x_all[s, q, :, cols] = quarter[s]
+    pl.loop(0, n_c // 2)(factors)
     for c in stage:
         c.wait()
     stage = []
@@ -160,14 +181,10 @@
         )
         stage[-1].start()
 
-    @pl.loop(0, n_c)
-    def _(j):
-        for c in pre_copies(j):
-            c.start()
-
     for j in range(min(SLOTS, n_c)):
         for c in w_copies(j):
             c.start()
+    pl.loop(n_c // 2, n_c)(factors)
     for c in stage:
         c.wait()
     swap = remote(x_all.at[:, :, :, cols], x_all.at[:, :, :, cols], sem_d, (0,), {"tp": mate})
@@ -194,8 +211,7 @@
     def send_l(j):
         return remote(to_l.at[j], from_r.at[j], sem_l, (j,), {"sp": jnp.maximum(s - 1, 0)})
 
-    @pl.loop(0, n_c)
-    def _(j):
+    def partial(j):
         wd_copy(j).wait()
         p = lax.dot_general(
             x_flat[...], w_d[j], (((1,), (1,)), ((), ())), preferred_element_type=F32
@@ -214,24 +230,15 @@
             send_l(j).start()
             from_r[j] = jnp.zeros((tokens, chunk), BF)
 
-    for c in in_stage:
-        c.wait()
+    ahead = n_c // 2
+    pl.loop(0, ahead)(partial)
     in_swap = remote(in_all.at[:, k], in_all.at[:, k], sem_j, (0,), {"tp": mate})
-    in_swap.start()
-
-    lag = jnp.maximum(s - 1, n_s - 2 - s)
+    lag = SLACK * jnp.maximum(s - 1, n_s - 2 - s)
 
     def finish(f):
-        for c in pre_copies(f):
-            c.wait()
         h = part[f] + from_l[f].astype(F32) + from_r[f].astype(F32)
-        gate = gates[f].astype(F32)
-        upward = ups[f].astype(F32)
-        sigmoid = 1.0 / (1.0 + jnp.exp(-gate))
-        swish = gate * sigmoid
-        gg[f] = (h * upward * sigmoid * (1.0 + gate * (1.0 - sigmoid))).astype(BF)
-        ug[f] = (h * swish).astype(BF)
-        hid[f] = (swish * upward).astype(BF).T
+        gg[f] = (h * slopes[f]).astype(BF)
+        ug[f] = (h * swishes[f]).astype(BF)
         for c in out_copies(f):
             c.start()
         for c in w_copies(f):
@@ -254,10 +261,10 @@
             for c in w_copies(f + SLOTS):
                 c.start()
 
-    @pl.loop(0, n_c + n_s - 2)
+    @pl.loop(0, n_c + SLACK * (n_s - 2))
     def _(step):
-        cr = step - (s - 1)
-        cl = step - (n_s - 2 - s)
+        cr = step - SLACK * (s - 1)
+        cl = step - SLACK * (n_s - 2 - s)
         f = step - lag
 
         @pl.when((s > 0) & (cr >= 0) & (cr < n_c))
@@ -278,6 +285,16 @@
                 to_l[cl] = (part[cl] + from_r[cl].astype(F32)).astype(BF)
                 send_l(cl).start()
 
+        @pl.when(step < n_c - ahead)
+        def _():
+            partial(step + ahead)
+
+        @pl.when(step == 1)
+        def _():
+            for c in in_stage:
+                c.wait()
+            in_swap.start()
+
         @pl.when((f >= 0) & (f < n_c))
         def _():
             finish(f)
@@ -305,6 +322,7 @@
     def _(j):
         for c in out_copies(j):
             c.wait()
+        hid_copy(j).wait()
 
         @pl.when(s < n_s - 1)
         def _():
@@ -356,6 +374,8 @@
         vm((n_c, tokens, chunk), BF),
         vm((n_c, tokens, chunk), BF),
         vm((n_c, tokens, chunk), BF),
+        vm((n_c, tokens, chunk), F32),
+        vm((n_c, tokens, chunk), F32),
         vm((n_c, tokens, chunk), BF),
         vm((n_c, tokens, chunk), BF),
         vm((n_c, chunk, tokens), BF),

time: 119 us -> 108 us (0.908)
  Pallas kernels: 117 us -> 107 us
    pallas_call x1, Pallas kernels: 98.5 us -> 88.2 us  [fused(): pl.pallas_call(functools.partial(first_kernel, n_q, n_s, chunk, n_c, tile...]
where the time goes in v2:
time: 108 us
  Pallas kernels  107 us (99%)
    pallas_call x1, Pallas kernels, fused(): pl.pallas_call(functools.partial(first_kernel, n_q, n_s, chunk, n_c, tile...  88.2 us
    pallas_call x1, Pallas kernels, fused(): pl.pallas_call(functools.partial(second_kernel, n_sub, chunk), grid=(n_c...  18.6 us

profile of v2, /device:TPU:0, one launch (start us, length us, event | category | flops | bytes accessed | tf_op | source)
XLA Modules:
  0.0 108.1 jit_solution(6352663109494160458)
XLA Ops:
  0.6 88.2 %shard_map.102 = (bf16[32,2048]{1,0:T(8,128)(2,1)}, bf16[256,2048]{1,0:T(8,128)(2,1)}, bf16[2048,256]{1,0:T(8,128)(2,1)}, bf16[14,256,256]{2,1,0:T(8,128)(2,1)},...) custom-call(bf16[32,2048]{1,0:T(8,128)(2,1)} %inputs.1, bf16[64,1024]{1,0:T(8,128)(2,1)} %out_grad.1, ...), custom_call_target="tpu_custom_call" | custom-call | flops 11274289152 | bytes 56885248 | tf_op jit(solution)/shard_map/pallas_call | solution.py:402
  88.8 0.0 copy-start
  88.8 18.6 %shard_map.103 = (bf16[2048,3584]{1,0:T(8,128)(2,1)}, bf16[2048,3584]{1,0:T(8,128)(2,1)}, bf16[3584,2048]{1,0:T(8,128)(2,1)}) custom-call(bf16[256,2048]{1,0:T(8,128)(2,1)} %get-tuple-element.14.x, bf16[2048,256]{1,0:T(8,128)(2,1)} %get-tuple-element.15.in_t, bf16[14,256,256]{2,1,0:T(8,128)(2,1)} %get-tuple-element.16.gg, ...), custom_call_target="tpu_custom_call" | custom-call | flops 11274289152 | bytes 49545216 | tf_op jit(solution)/shard_map/pallas_call | solution.py:428
  107.4 0.0 copy-done
  107.4 0.7 copy.12
Async XLA Ops:
  88.8 18.6 %copy-start = (bf16[32,2048]{1,0:T(8,128)(2,1)S(1)}, bf16[32,2048]{1,0:T(8,128)(2,1)}, u32[]{:S(2)}) copy-start(bf16[32,2048]{1,0:T(8,128)(2,1)} %get-tuple-element.26) | copy-start | bytes 393220
